TPU v7x, 256 devices: a whole 4x4x8 slice. The times are simulated.
256 devices in a mesh: node: 32 (over z, x_lo, core), local: 8 (over x_hi, y).
Axes of the slice: x: 4 (x_hi: 2, x_lo: 2; x = x_hi * 2 + x_lo), y: 4, z: 8, core: 2. Of those that a mesh axis runs over, the one named last changes fastest.
Arguments:
- tokens: bfloat16 [4096, 10240], P('node'), may hold values from -6 to 6
- master: float32 [10240, 10240], P('node', 'local'), may hold values from -0.0625 to 0.0625
- moment_one: float32 [10240, 10240], P('node', 'local'), may hold values from -6 to 6
- moment_two: float32 [10240, 10240], P('node', 'local'), may hold values from 0.5 to 20
- keys: bfloat16 [4096, 1024], P('node', 'local'), may hold values from -60 to 60
- values: bfloat16 [4096, 1024], P('node', 'local'), may hold values from -6 to 6
- d_context: bfloat16 [4096, 10240], P('node', 'local'), may hold values from -6 to 6
Outputs:
- context: bfloat16 [4096, 10240], P('node', 'local')
- d_keys: bfloat16 [4096, 1024], P('node', 'local')
- d_values: bfloat16 [4096, 1024], P('node', 'local')
- d_tokens: bfloat16 [4096, 10240], P(('node', 'local'))
- new_master: float32 [10240, 10240], P('node', 'local')
- new_moment_one: float32 [10240, 10240], P('node', 'local')
- new_moment_two: float32 [10240, 10240], P('node', 'local')
All inputs are finite; a program needn't handle non-finite values.
Results may differ from a plain program's by a relative error of at most 0.04.
The roundings to bfloat16 on the way count: a program that leaves them out, or rounds other values in their place, can miss the bound.
Values may be sent and summed in bfloat16 or wider, within the bound.
A program may use at most 192 MiB of HBM per device.

v0:
```python
import jax
import jax.numpy as jnp
from jax import lax
from jax.sharding import PartitionSpec as P

HS = 128


def adam_piece(master, moment_one, moment_two, gradient):
    new_one = 0.9 * moment_one + 0.1 * gradient
    new_two = 0.999 * moment_two + 0.001 * gradient * gradient
    first_hat = new_one / (1.0 - 0.9**10)
    second_hat = new_two / (1.0 - 0.999**10)
    new_master = master - 0.001 * first_hat / (jnp.sqrt(second_hat) + 1e-08)
    return (new_master, new_one, new_two)


def body(tokens, master, moment_one, moment_two, keys, values, d_context):
    weight_shard = master.astype(jnp.bfloat16)
    weight = lax.all_gather(weight_shard, "node", axis=0, tiled=True)
    length = tokens.shape[0]
    group_cols = weight.shape[1]
    heads = group_cols // HS
    scale = 1.0 / HS**0.5
    queries = jnp.dot(tokens, weight, preferred_element_type=jnp.float32).astype(jnp.bfloat16)
    query_heads = queries.reshape(length, heads, HS)
    scores = (
        jnp.einsum("qhd,kd->hqk", query_heads, keys, preferred_element_type=jnp.float32) * scale
    )
    rows_idx = lax.broadcasted_iota(jnp.int32, (length, length), 0)
    cols_idx = lax.broadcasted_iota(jnp.int32, (length, length), 1)
    scores = jnp.where((cols_idx <= rows_idx)[None], scores, jnp.float32(-1e30))
    probs = jax.nn.softmax(scores, axis=-1)
    probs_low = probs.astype(jnp.bfloat16)
    context = jnp.einsum("hqk,kd->qhd", probs_low, values, preferred_element_type=jnp.float32)
    context = context.astype(jnp.bfloat16).reshape(length, group_cols)
    grad_heads = d_context.reshape(length, heads, HS)
    d_probs = jnp.einsum("qhd,kd->hqk", grad_heads, values, preferred_element_type=jnp.float32)
    inner = jnp.sum(d_probs * probs, axis=-1, keepdims=True)
    d_scores = (probs * (d_probs - inner) * scale).astype(jnp.bfloat16)
    d_values = jnp.einsum(
        "hqk,qhd->kd", probs_low, grad_heads, preferred_element_type=jnp.float32
    ).astype(jnp.bfloat16)
    d_keys = jnp.einsum(
        "hqk,qhd->kd", d_scores, query_heads, preferred_element_type=jnp.float32
    ).astype(jnp.bfloat16)
    d_queries = jnp.einsum("hqk,kd->qhd", d_scores, keys, preferred_element_type=jnp.float32)
    d_queries = d_queries.astype(jnp.bfloat16).reshape(length, group_cols)
    grad_block = d_queries
    d_tokens = lax.psum_scatter(
        lax.dot_general(
            grad_block, weight, (((1,), (1,)), ((), ())), preferred_element_type=jnp.float32
        ).astype(jnp.bfloat16),
        "local",
        scatter_dimension=0,
        tiled=True,
    )
    grad_block = d_queries
    gradient = lax.psum_scatter(
        lax.dot_general(
            tokens, grad_block, (((0,), (0,)), ((), ())), preferred_element_type=jnp.float32
        ).astype(jnp.bfloat16),
        "node",
        scatter_dimension=0,
        tiled=True,
    ).astype(jnp.float32)
    new_master, new_one, new_two = adam_piece(master, moment_one, moment_two, gradient)
    return (context, d_keys, d_values, d_tokens, new_master, new_one, new_two)


def solution(mesh):
    return jax.shard_map(
        body,
        mesh=mesh,
        in_specs=(
            P("node", None),
            P("node", "local"),
            P("node", "local"),
            P("node", "local"),
            P("node", "local"),
            P("node", "local"),
            P("node", "local"),
        ),
        out_specs=(
            P("node", "local"),
            P("node", "local"),
            P("node", "local"),
            P(("node", "local"), None),
            P("node", "local"),
            P("node", "local"),
            P("node", "local"),
        ),
        check_vma=False,
    )
```

profile of v0, /device:TPU:32, one launch (start us, length us, event | category | flops | bytes accessed | tf_op | source)
XLA Modules:
  0.0 601.6 jit_solution(14559494507639220395)
XLA Ops:
  7.2 0.0 copy-start
  7.2 0.0 copy-start.2
  7.2 0.0 copy-start.4
  7.2 0.0 all-gather.2.cloned.1.call-start
  7.2 2.6 convert_element_type.42
  9.8 0.0 all-gather.2.cloned.1.call-update
  9.8 0.0 reduce-scatter.7.cloned.1.call-start
  9.9 0.0 copy-done.2
  9.9 0.2 copy.50
  10.1 0.0 copy-done.4
  10.1 1.1 convolution_bitcast_fusion
  11.2 0.0 copy-start.5
  11.2 149.1 %all-gather.2.cloned.1.call-done = bf16[10240,1280]{1,0:T(8,128)(2,1)} async-done(((bf16[320,1280]{1,0:T(8,128)(2,1)}), bf16[10240,1280]{1,0:T(8,128)(2,1)}) %all-gather.2.cloned.1.call-update) | async-done | bytes 26214416 | tf_op jit(solution)/shard_map/all_gather | solution.py:20
  160.4 0.0 copy-done
  160.4 10.4 %convolution_convert_fusion.2 = bf16[128,1280]{1,0:T(8,128)(2,1)S(1)} fusion(bf16[128,10240]{1,0:T(8,128)(2,1)S(1)} %copy-done, bf16[10240,1280]{1,0:T(8,128)(2,1)} %all-gather.2.cloned.1.call-done), kind=kOutput, calls=%fused_computation.7 | convolution fusion | flops 3355607040 | bytes 29163520 | tf_op jit(solution)/shard_map/dot_general | solution.py:25
  170.7 0.9 copy.46
  171.6 0.0 copy-done.5
  171.6 2.1 fusion.48
  173.8 2.0 convolution_convert_fusion.3
  175.8 12.3 %fusion.2 = bf16[10240,1280]{0,1:T(8,128)(2,1)} fusion(bf16[128,1280]{0,1:T(8,128)(2,1)S(1)} %bitcast.76, bf16[128,10240]{1,0:T(8,128)(2,1)S(1)} %copy-done), kind=kOutput, calls=%fused_computation.3 | convolution fusion | flops 3368550400 | bytes 29163520 | tf_op jit(solution)/shard_map/dot_general | solution.py:60
  188.1 32.3 %copy.73 = bf16[10240,1280]{1,0:T(8,128)(2,1)} copy(bf16[10240,1280]{0,1:T(8,128)(2,1)} %fusion.2) | data formatting | bytes 52428800
  220.5 0.0 reduce-scatter.7.cloned.1.call-update
  220.5 0.2 reduce-scatter.5.cloned.1.call-start
  220.7 14.6 %convolution_convert_fusion.1 = bf16[128,10240]{1,0:T(8,128)(2,1)} fusion(bf16[128,1280]{0,1:T(8,128)(2,1)S(1)} %bitcast.77, bf16[10240,1280]{1,0:T(8,128)(2,1)} %all-gather.2.cloned.1.call-done), kind=kOutput, calls=%fused_computation.4 | convolution fusion | flops 3356753920 | bytes 29163520 | tf_op jit(solution)/shard_map/dot_general | solution.py:51
  235.3 0.0 reduce-scatter.5.cloned.1.call-update
  235.3 1.8 copy.58
  237.1 2.9 copy.56
  240.0 0.0 copy-start.3
  240.0 2.8 copy.57
  242.8 0.0 copy-done.3
  242.8 0.5 convolution_convert_fusion.4
  243.3 0.9 copy.59
  244.3 2.7 fusion.13
  246.9 1.1 fusion.14
  248.0 255.8 %reduce-scatter.7.cloned.1.call-done = bf16[320,1280]{1,0:T(8,128)(2,1)} async-done(((bf16[10240,1280]{1,0:T(8,128)(2,1)}), bf16[320,1280]{1,0:T(8,128)(2,1)}) %reduce-scatter.7.cloned.1.call-update) | async-done | bytes 819216
  503.9 2.2 copy.74
  506.1 5.8 divide_subtract_fusion
  511.8 2.7 copy.60
  514.6 0.0 copy-start.1
  514.6 2.9 copy.61
  517.5 2.7 copy.62
  520.2 74.8 %reduce-scatter.5.cloned.1.call-done = bf16[16,10240]{1,0:T(8,128)(2,1)} async-done(((bf16[128,10240]{1,0:T(8,128)(2,1)}), bf16[16,10240]{1,0:T(8,128)(2,1)}) %reduce-scatter.5.cloned.1.call-update) | async-done | bytes 327696 | tf_op jit(solution)/shard_map/reduce_scatter | solution.py:50
  595.0 0.0 copy-done.1
  (1 shorter events, 0.0 us)
Async XLA Ops:
  7.2 153.2 %copy-start = (bf16[128,10240]{1,0:T(8,128)(2,1)S(1)}, bf16[128,10240]{1,0:T(8,128)(2,1)}, u32[]{:S(2)}) copy-start(bf16[128,10240]{1,0:T(8,128)(2,1)} %param.7) | copy-start | bytes 7864324
  7.2 2.7 copy-start.2
  7.2 2.9 copy-start.4
  7.2 153.2 %all-gather.2.cloned.1.call-start = ((), (), s32[]{:S(2)}) async-start(), calls=%async_computation.2 | async-start | bytes 27033600 | tf_op jit(solution)/shard_map/all_gather | solution.py:20
  9.8 494.0 %reduce-scatter.7.cloned.1.call-start = ((), (), s32[]{:S(2)}) async-start(), calls=%async_computation.4 | async-start | bytes 27033600
  11.2 160.4 %copy-start.5 = (bf16[128,128]{1,0:T(8,128)(2,1)S(1)}, bf16[128,128]{1,0:T(8,128)(2,1)}, u32[]{:S(2)}) copy-start(bf16[128,128]{1,0:T(8,128)(2,1)} %param.11) | copy-start | bytes 98308
  220.5 374.6 %reduce-scatter.5.cloned.1.call-start = ((), (), s32[]{:S(2)}) async-start(), calls=%async_computation.3 | async-start | bytes 2949120 | tf_op jit(solution)/shard_map/reduce_scatter | solution.py:50
  240.0 2.8 copy-start.3
  514.6 80.5 %copy-start.1 = (bf16[128,10240]{1,0:T(8,128)(2,1)S(1)}, bf16[128,10240]{1,0:T(8,128)(2,1)}, u32[]{:S(2)}) copy-start(bf16[128,10240]{1,0:T(8,128)(2,1)} %param.7) | copy-start | bytes 7864324
Sparse Core Ops, SparseCore 0:
  10.5 149.8 all-gather.1
  220.6 283.2 reduce-scatter.6
  508.5 86.4 reduce-scatter.4
where the time goes:
time: 603 us; the launch traced here: 602 us
  waiting for transfers between devices  480 us (80%)
  local copies, waits for them, and re-layouts  52.4 us (9%)
  matrix products  46.8 us (8%)
  between operations  13.8 us (2%)
  other arithmetic  8.36 us (1%)
    unnamed x4, waiting for transfers between devices  256 us
    all_gather x1, waiting for transfers between devices, body(): weight = lax.all_gather(weight_shard, 'node', axis=0, tiled=True)  149 us
    reduce_scatter x1, waiting for transfers between devices, body(): lax.psum_scatter(lax.dot_general(grad_block, weight, (((1,), (1,)), ((),...  74.8 us
    unnamed x22, local copies, waits for them, and re-layouts  51.5 us
    dot_general x1, matrix products, body(): lax.dot_general(grad_block, weight, (((1,), (1,)), ((), ())), preferred_e...  14.6 us
    dot_general x1, matrix products, body(): lax.dot_general(tokens, grad_block, (((0,), (0,)), ((), ())), preferred_e...  12.3 us
  transfers between devices with their start and end apart: 3, of which 3 were waited for; matrix products, arithmetic and copies ran while one was open for 7% of the time, Pallas kernels for 0%

commit v1 on v0

v1 whole, which is shorter than its diff:
```python
import functools

import jax
import jax.numpy as jnp
from jax import lax
from jax.experimental import pallas as pl
from jax.experimental.pallas import tpu as pltpu
from jax.sharding import PartitionSpec as P

MESH = pl.DeviceIdType.MESH
HS = 128
NZ, NY = 8, 4
PW = 2 * HS
ORDER = (4, 3, 5, 2, 6, 1, 7)
F32, BF16 = jnp.float32, jnp.bfloat16


def adam_piece(master, moment_one, moment_two, gradient):
    new_one = 0.9 * moment_one + 0.1 * gradient
    new_two = 0.999 * moment_two + 0.001 * gradient * gradient
    first_hat = new_one / (1.0 - 0.9**10)
    second_hat = new_two / (1.0 - 0.999**10)
    new_master = master - 0.001 * first_hat / (jnp.sqrt(second_hat) + 1e-08)
    return (new_master, new_one, new_two)


def dot(a, b, dims=((1,), (0,))):
    return lax.dot_general(a, b, (dims, ((), ())), preferred_element_type=F32)


def kernel(
    tokens_ref, master_ref, keys_ref, values_ref, dctx_ref,
    ctx_ref, dk_ref, dv_ref, dtok_ref, grad_ref,
    tok, tok_t, wg, part, ring, dqall, dk_acc, dv_acc, dacc, dts, yr2, yr1, red, xr, fin, dtk,
    ga, gs, gcr, gxs, gxr,
    own_sem, w_s, w_r, tz_s, tz_r, ty_s, ty_r, rs_s, rs_r, ag_s, ag_r, y_s, y_r, x_s, x_r, zd_s, zd_r,
    gc_s, gc_r, gx_s, gx_r,
):
    length = keys_ref.shape[0]
    rows, cols = master_ref.shape
    depth = 4 * rows
    pairs = cols // PW
    node, local = lax.axis_index("node"), lax.axis_index("local")
    z, r = node // 4, node % 4
    xl, c = r // 2, r % 2
    xh, y = local // NY, local % NY
    quarter = length // NY
    half_rows = quarter // 2

    def plane(offset):
        return (z + offset + NZ) % NZ

    def at_z(where):
        return {"node": where * 4 + r, "local": local}

    def at_y(where):
        return {"node": node, "local": xh * NY + where}

    z_up, z_dn = at_z(plane(1)), at_z(plane(-1))
    yp, ym, y2 = (y + 1) % NY, (y + 3) % NY, (y + 2) % NY
    y_up, y_dn = at_y(yp), at_y(ym)
    other_core = {"node": z * 4 + xl * 2 + (1 - c), "local": local}
    other_xl = {"node": z * 4 + (1 - xl) * 2 + c, "local": local}
    other_xh = {"node": node, "local": (1 - xh) * NY + y}

    def remote(src, dst, send_sem, recv_sem, device):
        return pltpu.make_async_remote_copy(
            src_ref=src, dst_ref=dst, send_sem=send_sem, recv_sem=recv_sem,
            device_id=device, device_id_type=MESH,
        )

    barrier = pltpu.get_barrier_semaphore()
    partners = [at_z(plane(d)) for d in range(1, NZ)] + [y_up, y_dn, other_core, other_xl, other_xh]
    for device in partners:
        pl.semaphore_signal(barrier, inc=1, device_id=device, device_id_type=MESH)
    pl.semaphore_wait(barrier, len(partners))

    def row_block(base, count):
        return pl.ds(pl.multiple_of(base, 16), count)

    def token_out(j):
        to = plane(ORDER[j])
        src = tokens_ref.at[row_block(y * quarter, quarter), pl.ds(pl.multiple_of(to * depth, 128), depth)]
        return remote(src, tok.at[z, row_block(y * quarter, quarter), :], tz_s.at[j], tz_r.at[j], at_z(to))

    def token_in(j):
        block = tok.at[plane(-ORDER[j]), row_block(y * quarter, quarter), :]
        return remote(block, block, tz_s.at[j], tz_r.at[j], z_up)

    def token_y(j, kind, incoming):
        s = plane(-ORDER[j])
        me = (yp if kind in (1, 3) else ym) if incoming else y
        base, count = me * quarter, quarter
        if kind >= 2:
            origin = y2 if incoming else (ym if kind == 2 else yp)
            base, count = origin * quarter + (0 if kind == 2 else half_rows), half_rows
        block = tok.at[s, row_block(base, count), :]
        return remote(block, block, ty_s.at[kind, j], ty_r.at[kind, j], y_up if kind in (0, 2) else y_dn)

    for j in range(NZ - 1):
        token_out(j).start()
    own_tokens = pltpu.make_async_copy(
        tokens_ref.at[:, pl.ds(pl.multiple_of(z * depth, 128), depth)], tok.at[z], own_sem
    )
    own_tokens.start()

    def w_block(k, which):
        return wg.at[k, pl.ds(pl.multiple_of(which * rows, 64), rows), :]

    def w_copy(kind, k, incoming):
        sent = (r, r, r ^ 2)[kind]
        came = (r ^ 1, r ^ 2, r ^ 3)[kind]
        block = w_block(k, came if incoming else sent)
        return remote(block, block, w_s.at[kind, k], w_r.at[kind, k], other_xl if kind == 1 else other_core)

    for k in range(pairs):
        wg[k, pl.ds(pl.multiple_of(r * rows, 64), rows), :] = master_ref[:, k * PW : (k + 1) * PW].astype(BF16)
        w_copy(1, k, False).start()
        w_copy(0, k, False).start()

    def hand_on(j):
        token_y(j, 0, True).wait_recv()
        token_y(j, 2, False).start()
        token_y(j, 1, True).wait_recv()
        token_y(j, 3, False).start()

    for j in range(NZ - 1):
        token_in(j).wait_recv()
        token_y(j, 0, False).start()
        token_y(j, 1, False).start()
        if j < pairs:
            w_copy(1, j, True).wait_recv()
            w_copy(2, j, False).start()
        if j >= 1:
            hand_on(j - 1)
    hand_on(NZ - 2)
    own_tokens.wait()
    for j in range(NZ - 1):
        token_y(j, 2, True).wait_recv()
        token_y(j, 3, True).wait_recv()

    def rs_copy(way, d, k):
        sign = 1 if way == 0 else -1
        src = part.at[k, plane(sign * d)]
        dst = ring.at[way, d - 1, k]
        if d == 4:
            src, dst = src.at[way], dst.at[way]
        return remote(src, dst, rs_s.at[way, d - 1, k], rs_r.at[way, d - 1, k], z_up if way == 0 else z_dn)

    def gemm_step(k, carry):
        w_copy(0, k, True).wait_recv()
        w_copy(2, k, True).wait_recv()
        out = dot(tok[...].reshape(NZ * length, depth), wg[k])
        for t in range(NZ):
            for a in range(2):
                part[k, t, a] = out[t * length : (t + 1) * length, a * HS : (a + 1) * HS]
        for way in range(2):
            rs_copy(way, 4, k).start()
        return carry

    lax.fori_loop(0, pairs, gemm_step, 0)
    for d in (3, 2, 1):

        def ring_step(k, carry, d=d):
            for way in range(2):
                rs_copy(way, d + 1, k).wait_recv()
                t = plane(d if way == 0 else -d)
                if d == 3:
                    part[k, t, way] += ring[way, d, k, way]
                else:
                    part[k, t] += ring[way, d, k]
                rs_copy(way, d, k).start()
            return carry

        lax.fori_loop(0, pairs, ring_step, 0)

    def transpose_step(s, carry):
        tok_t[:, pl.ds(pl.multiple_of(s * length, 128), length)] = tok[s].T
        return carry

    lax.fori_loop(0, NZ, transpose_step, 0)

    scale = 1.0 / HS**0.5
    row_id = lax.broadcasted_iota(jnp.int32, (length, length), 0)
    col_id = lax.broadcasted_iota(jnp.int32, (length, length), 1)
    causal = col_id <= row_id
    dk_acc[...] = jnp.zeros_like(dk_acc)
    dv_acc[...] = jnp.zeros_like(dv_acc)

    def ag_copy(way, d, k, incoming):
        sign = -1 if way == 0 else 1
        block = dqall.at[k, plane(sign * (d if incoming else d - 1))]
        if d == 4:
            block = block.at[:, pl.ds(way * HS, HS)]
        return remote(block, block, ag_s.at[way, d - 1, k], ag_r.at[way, d - 1, k], z_up if way == 0 else z_dn)

    def attention_step(k, carry):
        for way in range(2):
            rs_copy(way, 1, k).wait_recv()
        keys, values = keys_ref[...], values_ref[...]
        lanes = pl.ds(pl.multiple_of(k * PW, 128), PW)
        grads = dctx_ref[:, lanes]
        ctx, dq = [], []
        dk, dv = dk_acc[...], dv_acc[...]
        for a in range(2):
            q = (part[k, z, a] + ring[0, 0, k, a] + ring[1, 0, k, a]).astype(BF16)
            g = grads[:, a * HS : (a + 1) * HS]
            scores = jnp.where(causal, dot(q, keys, ((1,), (1,))) * scale, -1e30)
            e = jnp.exp(scores - jnp.max(scores, axis=-1, keepdims=True))
            probs = e * (1.0 / jnp.sum(e, axis=-1, keepdims=True))
            low = probs.astype(BF16)
            ctx.append(dot(low, values).astype(BF16))
            d_probs = dot(g, values, ((1,), (1,)))
            inner = jnp.sum(d_probs * probs, axis=-1, keepdims=True)
            ds = (probs * (d_probs - inner) * scale).astype(BF16)
            dv = dv + dot(low, g, ((0,), (0,)))
            dk = dk + dot(ds, q, ((0,), (0,)))
            dq.append(dot(ds, keys).astype(BF16))
        dk_acc[...], dv_acc[...] = dk, dv
        ctx_ref[:, lanes] = jnp.concatenate(ctx, axis=1)
        dqall[k, z] = jnp.concatenate(dq, axis=1)
        for way in range(2):
            ag_copy(way, 1, k, False).start()
        return carry

    lax.fori_loop(0, pairs, attention_step, 0)
    dk_ref[...] = dk_acc[...].astype(BF16)
    dv_ref[...] = dv_acc[...].astype(BF16)

    groups = [(0, 1), (1, 2), (3, 2), (5, 2), (7, 1)]
    offsets = (0, -1, 1, -2, 2, -3, 3, 4)
    mid = cols // 2

    def y_copy(g, way, d):
        first, count = groups[g]
        slots = pl.ds(first, count)
        if d == 2:
            src = dts.at[slots, y2, :, pl.ds(way * mid, mid)]
            dst = yr2.at[way, slots]
        else:
            src = dts.at[slots, yp if way == 0 else ym]
            dst = yr1.at[way, slots]
        return remote(src, dst, y_s.at[way, d - 1, g], y_r.at[way, d - 1, g], y_up if way == 0 else y_dn)

    def accumulate(g, k):
        first, count = groups[g]
        lhs = jnp.concatenate([dqall[k, plane(offsets[first + i])] for i in range(count)], axis=0)
        return dot(lhs, wg[k], ((1,), (1,)))

    def gemm_out(g, total):
        first, count = groups[g]
        for i in range(count):
            for owner in range(2 * NY):
                block = total[i * length + owner * 16 : i * length + (owner + 1) * 16]
                dts[first + i, owner % NY, (owner // NY) * 16 : (owner // NY + 1) * 16] = block.astype(BF16)
        for way in range(2):
            y_copy(g, way, 2).start()

    def y_first(g):
        first, count = groups[g]
        for way in range(2):
            y_copy(g, way, 2).wait_recv()
            to = yp if way == 0 else ym
            for i in range(count):
                own = dts[first + i, to, :, way * mid : (way + 1) * mid].astype(F32)
                came = yr2[way, first + i].astype(F32)
                dts[first + i, to, :, way * mid : (way + 1) * mid] = (own + came).astype(BF16)
            y_copy(g, way, 1).start()

    def x_copy(g):
        first, count = groups[g]
        slots = pl.ds(first, count)
        return remote(red.at[slots, 1 - xh], xr.at[slots], x_s.at[g], x_r.at[g], other_xh)

    def y_second(g):
        first, count = groups[g]
        for way in range(2):
            y_copy(g, way, 1).wait_recv()
        for i in range(count):
            slot = first + i
            total = dts[slot, y].astype(F32) + yr1[0, slot].astype(F32) + yr1[1, slot].astype(F32)
            for side in range(2):
                red[slot, side] = total[side * 16 : (side + 1) * 16].astype(BF16)
        x_copy(g).start()

    def home_copy(slot):
        block = dtk.at[:, pl.ds(pl.multiple_of(z * depth, 128), depth)]
        return remote(fin.at[slot], block, zd_s.at[slot], zd_r.at[slot], at_z(plane(offsets[slot])))

    def home_in(slot):
        block = dtk.at[:, pl.ds(pl.multiple_of(plane(-offsets[slot]) * depth, 128), depth)]
        return remote(fin.at[slot], block, zd_s.at[slot], zd_r.at[slot], z_up)

    def x_done(g):
        first, count = groups[g]
        x_copy(g).wait_recv()
        for i in range(count):
            slot = first + i
            total = (red[slot, xh].astype(F32) + xr[slot].astype(F32)).astype(BF16)
            if slot == 0:
                dtk[:, pl.ds(pl.multiple_of(z * depth, 128), depth)] = total
            else:
                fin[slot] = total
                home_copy(slot).start()

    dacc[...] = jnp.zeros_like(dacc)

    def own_step(k, carry):
        dacc[:length] += accumulate(0, k)
        return carry

    lax.fori_loop(0, pairs, own_step, 0)
    gemm_out(0, dacc[:length])
    for d in (1, 2, 3):
        dacc[...] = jnp.zeros_like(dacc)

        def gather_step(k, carry, d=d):
            for way in range(2):
                ag_copy(way, d, k, True).wait_recv()
                ag_copy(way, d + 1, k, False).start()
            dacc[...] += accumulate(d, k)
            return carry

        lax.fori_loop(0, pairs, gather_step, 0)
        gemm_out(d, dacc[...])
        y_first(d - 1)
        if d >= 2:
            y_second(d - 2)
        if d >= 3:
            x_done(d - 3)

    def gc_copy(k):
        return remote(gs.at[k], gcr.at[k], gc_s.at[k], gc_r.at[k], other_core)

    def gx_copy(k):
        return remote(gxs.at[k], gxr.at[k], gx_s.at[k], gx_r.at[k], other_xl)

    def own_rows(side, core):
        return pl.ds(pl.multiple_of((side * 2 + core) * rows, 64), rows)

    def core_sum(k):
        gc_copy(k).wait_recv()
        away = 1 - xl
        gxs[k] = (ga[k, own_rows(away, c), :] + gcr[k, away].astype(F32)).astype(BF16)
        gx_copy(k).start()

    def grad_step(k, carry):
        for way in range(2):
            ag_copy(way, 4, k, True).wait_recv()
        ga[k] = dot(tok_t[...], dqall[k].reshape(NZ * length, PW))
        for side in range(2):
            gs[k, side] = ga[k, own_rows(side, 1 - c), :].astype(BF16)
        gc_copy(k).start()

        @pl.when(k >= 1)
        def _():
            core_sum(k - 1)

        return carry

    lax.fori_loop(0, pairs, grad_step, 0)
    core_sum(pairs - 1)

    dacc[...] = jnp.zeros_like(dacc)

    def last_step(k, carry):
        dacc[:length] += accumulate(4, k)
        return carry

    lax.fori_loop(0, pairs, last_step, 0)
    gemm_out(4, dacc[:length])
    y_first(3)
    y_second(2)
    x_done(1)
    y_first(4)
    y_second(3)
    x_done(2)
    y_second(4)
    x_done(3)
    x_done(4)

    for k in range(pairs):
        gx_copy(k).wait_recv()
        mine = ga[k, own_rows(xl, c), :] + gcr[k, xl].astype(F32) + gxr[k].astype(F32)
        grad_ref[:, k * PW : (k + 1) * PW] = mine
    for slot in range(1, NZ):
        home_in(slot).wait_recv()
    dtok_ref[...] = dtk[...]

    for j in range(NZ - 1):
        token_out(j).wait_send()
        for kind in range(4):
            token_y(j, kind, False).wait_send()

    def drain(k, carry):
        for kind in range(3):
            w_copy(kind, k, False).wait_send()
        for way in range(2):
            for d in range(1, 5):
                rs_copy(way, d, k).wait_send()
                ag_copy(way, d, k, False).wait_send()
        gc_copy(k).wait_send()
        gx_copy(k).wait_send()
        return carry

    lax.fori_loop(0, pairs, drain, 0)
    for g in range(len(groups)):
        for way in range(2):
            for d in (1, 2):
                y_copy(g, way, d).wait_send()
        x_copy(g).wait_send()
    for slot in range(1, NZ):
        home_copy(slot).wait_send()


def fused(tokens, master, keys, values, d_context):
    length, width = tokens.shape
    rows, cols = master.shape
    depth, pairs, mid, quarter = 4 * rows, cols // PW, cols // 2, length // NY
    vmem, dma = pltpu.VMEM, pltpu.SemaphoreType.DMA
    in_vmem = pl.BlockSpec(memory_space=pltpu.VMEM)
    return pl.pallas_call(
        kernel,
        out_shape=(
            jax.ShapeDtypeStruct((length, cols), BF16),
            jax.ShapeDtypeStruct((length, HS), BF16),
            jax.ShapeDtypeStruct((length, HS), BF16),
            jax.ShapeDtypeStruct((length // 8, width), BF16),
            jax.ShapeDtypeStruct((rows, cols), F32),
        ),
        in_specs=[pl.BlockSpec(memory_space=pl.ANY)] + [in_vmem] * 4,
        out_specs=[in_vmem] * 5,
        scratch_shapes=[
            vmem((NZ, length, depth), BF16),
            vmem((depth, NZ * length), BF16),
            vmem((pairs, depth, PW), BF16),
            vmem((pairs, NZ, 2, length, HS), F32),
            vmem((2, 4, pairs, 2, length, HS), F32),
            vmem((pairs, NZ, length, PW), BF16),
            vmem((length, HS), F32),
            vmem((length, HS), F32),
            vmem((2 * length, depth), F32),
            vmem((NZ, NY, quarter, depth), BF16),
            vmem((2, NZ, quarter, mid), BF16),
            vmem((2, NZ, quarter, depth), BF16),
            vmem((NZ, 2, 16, depth), BF16),
            vmem((NZ, 16, depth), BF16),
            vmem((NZ, 16, depth), BF16),
            vmem((length // 8, width), BF16),
            vmem((pairs, depth, PW), F32),
            vmem((pairs, 2, rows, PW), BF16),
            vmem((pairs, 2, rows, PW), BF16),
            vmem((pairs, rows, PW), BF16),
            vmem((pairs, rows, PW), BF16),
            dma,
            dma((3, pairs)), dma((3, pairs)),
            dma((NZ - 1,)), dma((NZ - 1,)),
            dma((4, NZ - 1)), dma((4, NZ - 1)),
            dma((2, 4, pairs)), dma((2, 4, pairs)),
            dma((2, 4, pairs)), dma((2, 4, pairs)),
            dma((2, 2, 5)), dma((2, 2, 5)),
            dma((5,)), dma((5,)),
            dma((NZ,)), dma((NZ,)),
            dma((pairs,)), dma((pairs,)),
            dma((pairs,)), dma((pairs,)),
        ],
        compiler_params=pltpu.CompilerParams(
            collective_id=0, has_side_effects=True, vmem_limit_bytes=60 * 1024 * 1024
        ),
    )(tokens, master, keys, values, d_context)


def body(tokens, master, moment_one, moment_two, keys, values, d_context):
    context, d_keys, d_values, d_tokens, gradient = fused(tokens, master, keys, values, d_context)
    new_master, new_one, new_two = adam_piece(master, moment_one, moment_two, gradient)
    return (context, d_keys, d_values, d_tokens, new_master, new_one, new_two)


def solution(mesh):
    both = P("node", "local")
    return jax.shard_map(
        body,
        mesh=mesh,
        in_specs=(P("node", None), both, both, both, both, both, both),
        out_specs=(both, both, both, P(("node", "local"), None), both, both, both),
        check_vma=False,
    )
```

time: 603 us -> 169 us (0.28)
  waiting for transfers between devices: 480 us -> 0 us
  Pallas kernels: 0 us -> 158 us
  local copies, waits for them, and re-layouts: 52.4 us -> 2.7 us
  matrix products: 46.8 us -> 0 us
  between operations: 13.8 us -> 0.71 us
    unnamed x4 -> x0, waiting for transfers between devices: 256 us -> none
    pallas_call x0 -> x1, Pallas kernels: none -> 158 us  [fused(): pl.pallas_call(kernel, out_shape=(jax.ShapeDtypeStruct((length, cols), BF...]
    all_gather x1 -> x0, waiting for transfers between devices: 149 us -> none  [body(): weight = lax.all_gather(weight_shard, 'node', axis=0, tiled=True)]
    reduce_scatter x1 -> x0, waiting for transfers between devices: 74.8 us -> none  [body(): lax.psum_scatter(lax.dot_general(grad_block, weight, (((1,), (1,)), ((),...]
    unnamed x22 -> x16, local copies, waits for them, and re-layouts: 51.5 us -> 2.7 us
    dot_general x8 -> x0, matrix products: 44.6 us -> none  [the longest x1 14.6 us: body(): lax.dot_general(grad_block, weight, (((1,), (1,)), ((), ())), preferred_e...]
  transfers between devices with their start and end apart: 3 -> 0, of which waited for: 3 -> 0; matrix products, arithmetic and copies ran while one was open for 7% -> 0% of each run, Pallas kernels for 0% -> 0%
where the time goes in v1:
time: 169 us; the launch traced here: 166 us
  Pallas kernels  158 us (93%)
  other arithmetic  4.81 us (3%)
  local copies, waits for them, and re-layouts  2.7 us (2%)
    pallas_call x1, Pallas kernels, fused(): pl.pallas_call(kernel, out_shape=(jax.ShapeDtypeStruct((length, cols), BF...  158 us
    sub x1, other arithmetic, adam_piece(): new_master = master - 0.001 * first_hat / (jnp.sqrt(second_hat) + 1e-08)  4.81 us

profile of v1, /device:TPU:32, one launch (start us, length us, event | category | flops | bytes accessed | tf_op | source)
XLA Modules:
  0.0 166.0 jit_solution(11966609108233880190)
XLA Ops:
  0.6 0.0 copy-start
  0.6 0.0 copy-start.1
  0.7 157.8 %shard_map.126 = (bf16[128,1280]{1,0:T(8,128)(2,1)}, bf16[128,128]{1,0:T(8,128)(2,1)}, bf16[128,128]{1,0:T(8,128)(2,1)}, bf16[16,10240]{1,0:T(8,128)(2,1)}, f32[320,1280]{1,0:T(8,128)}) custom-call(bf16[128,10240]{1,0:T(8,128)(2,1)} %tokens_ref.1, f32[320,1280]{1,0:T(8,128)} %master_ref.1, bf16[128,128]{1,0:T(8,128)(2,1)} %keys_ref.1, ...), custom_call_target="tpu_custom_call" | custom-call | tf_op jit(solution)/shard_map/pallas_call | solution.py:422
  158.4 0.0 copy-done
  158.4 0.0 copy-done.1
  158.4 0.0 copy-start.3
  158.5 0.0 copy-start.5
  158.5 0.0 copy-start.4
  158.5 0.0 copy-start.2
  158.5 4.8 %divide_subtract_fusion = (f32[320,1280]{1,0:T(8,128)}, f32[320,1280]{1,0:T(8,128)}, f32[320,1280]{1,0:T(8,128)}) fusion(f32[320,1280]{1,0:T(8,128)S(1)} %copy-done, f32[320,1280]{1,0:T(8,128)} %get-tuple-element.16, f32[320,1280]{1,0:T(8,128)S(1)} %copy-done.1, f32[320,1280]{1,0:T(8,128)} %param.10), kind=kLoop, calls=%fused_computation.2 | loop fusion | flops 4915200 | bytes 11468800 | tf_op jit(solution)/shard_map/sub | solution.py:23
  163.3 0.0 copy-done.3
  163.3 0.7 copy.18
  164.0 0.0 copy-done.5
  164.0 0.6 copy.19
  164.6 0.0 copy-done.4
  164.6 0.6 copy.20
  165.3 0.0 copy-done.2
  165.3 0.7 copy.21
Async XLA Ops:
  0.6 157.8 %copy-start = (f32[320,1280]{1,0:T(8,128)S(1)}, f32[320,1280]{1,0:T(8,128)}, u32[]{:S(2)}) copy-start(f32[320,1280]{1,0:T(8,128)} %master_ref.1) | copy-start | bytes 4915204
  0.6 157.8 %copy-start.1 = (f32[320,1280]{1,0:T(8,128)S(1)}, f32[320,1280]{1,0:T(8,128)}, u32[]{:S(2)}) copy-start(f32[320,1280]{1,0:T(8,128)} %param.9) | copy-start | bytes 4915204
  158.4 4.9 %copy-start.3 = (bf16[128,1280]{1,0:T(8,128)(2,1)S(1)}, bf16[128,1280]{1,0:T(8,128)(2,1)}, u32[]{:S(2)}) copy-start(bf16[128,1280]{1,0:T(8,128)(2,1)} %get-tuple-element.27) | copy-start | bytes 983044
  158.5 5.6 %copy-start.5 = (bf16[128,128]{1,0:T(8,128)(2,1)S(1)}, bf16[128,128]{1,0:T(8,128)(2,1)}, u32[]{:S(2)}) copy-start(bf16[128,128]{1,0:T(8,128)(2,1)} %get-tuple-element.28) | copy-start | bytes 98308
  158.5 6.2 %copy-start.4 = (bf16[128,128]{1,0:T(8,128)(2,1)S(1)}, bf16[128,128]{1,0:T(8,128)(2,1)}, u32[]{:S(2)}) copy-start(bf16[128,128]{1,0:T(8,128)(2,1)} %get-tuple-element.29) | copy-start | bytes 98308
  158.5 6.8 %copy-start.2 = (bf16[16,10240]{1,0:T(8,128)(2,1)S(1)}, bf16[16,10240]{1,0:T(8,128)(2,1)}, u32[]{:S(2)}) copy-start(bf16[16,10240]{1,0:T(8,128)(2,1)} %get-tuple-element.30) | copy-start | bytes 983044

commit v2 on v1

v2 whole, which is shorter than its diff:
```python
import functools

import jax
import jax.numpy as jnp
from jax import lax
from jax.experimental import pallas as pl
from jax.experimental.pallas import tpu as pltpu
from jax.sharding import PartitionSpec as P

MESH = pl.DeviceIdType.MESH
HS = 128
NZ, NY = 8, 4
PW = 2 * HS
ORDER = (4, 3, 5, 2, 6, 1, 7)
F32, BF16 = jnp.float32, jnp.bfloat16


def adam_piece(master, moment_one, moment_two, gradient):
    new_one = 0.9 * moment_one + 0.1 * gradient
    new_two = 0.999 * moment_two + 0.001 * gradient * gradient
    first_hat = new_one / (1.0 - 0.9**10)
    second_hat = new_two / (1.0 - 0.999**10)
    new_master = master - 0.001 * first_hat / (jnp.sqrt(second_hat) + 1e-08)
    return (new_master, new_one, new_two)


def dot(a, b, dims=((1,), (0,))):
    return lax.dot_general(a, b, (dims, ((), ())), preferred_element_type=F32)


def kernel(
    tokens_hbm, master_hbm, keys_hbm, values_hbm, dctx_hbm,
    ctx_hbm, dk_hbm, dv_hbm, dtok_hbm, grad_hbm,
    master_ref, keys_ref, values_ref, dctx_ref, ctx_ref, dk_ref, dv_ref, grad_ref,
    tok, tok_t, wg, wg_t, part, ring, dqall, dk_acc, dv_acc, d_probs_ref, low_ref, ds_ref, q_ref,
    dts, yr2, yr1, red, xr, fin, dtk,
    ga, gs, gcr, gxs, gxr,
    in_sem, out_sem, own_sem, w_s, w_r, tz_s, tz_r, ty_s, ty_r, rs_s, rs_r, ag_s, ag_r, y_s, y_r, x_s, x_r, zd_s, zd_r,
    gc_s, gc_r, gx_s, gx_r,
):
    length = keys_ref.shape[0]
    rows, cols = master_ref.shape
    depth = 4 * rows
    pairs = cols // PW
    node, local = lax.axis_index("node"), lax.axis_index("local")
    z, r = node // 4, node % 4
    xl, c = r // 2, r % 2
    xh, y = local // NY, local % NY
    quarter = length // NY
    half_rows = quarter // 2

    def plane(offset):
        return (z + offset + NZ) % NZ

    def at_z(where):
        return {"node": where * 4 + r, "local": local}

    def at_y(where):
        return {"node": node, "local": xh * NY + where}

    z_up, z_dn = at_z(plane(1)), at_z(plane(-1))
    yp, ym, y2 = (y + 1) % NY, (y + 3) % NY, (y + 2) % NY
    y_up, y_dn = at_y(yp), at_y(ym)
    other_core = {"node": z * 4 + xl * 2 + (1 - c), "local": local}
    other_xl = {"node": z * 4 + (1 - xl) * 2 + c, "local": local}
    other_xh = {"node": node, "local": (1 - xh) * NY + y}

    def remote(src, dst, send_sem, recv_sem, device):
        return pltpu.make_async_remote_copy(
            src_ref=src, dst_ref=dst, send_sem=send_sem, recv_sem=recv_sem,
            device_id=device, device_id_type=MESH,
        )

    barrier = pltpu.get_barrier_semaphore()
    partners = [at_z(plane(d)) for d in range(1, NZ)] + [y_up, y_dn, other_core, other_xl, other_xh]
    for device in partners:
        pl.semaphore_signal(barrier, inc=1, device_id=device, device_id_type=MESH)
    held = ((master_hbm, master_ref), (keys_hbm, keys_ref), (values_hbm, values_ref), (dctx_hbm, dctx_ref))
    loads = [pltpu.make_async_copy(src, dst, in_sem.at[i]) for i, (src, dst) in enumerate(held)]
    for load in loads:
        load.start()
    own_tokens = pltpu.make_async_copy(
        tokens_hbm.at[:, pl.ds(pl.multiple_of(z * depth, 128), depth)], tok.at[z], own_sem
    )
    own_tokens.start()
    loads[0].wait()
    for k in range(pairs):
        wg[k, pl.ds(pl.multiple_of(r * rows, 64), rows), :] = master_ref[:, k * PW : (k + 1) * PW].astype(BF16)
    pl.semaphore_wait(barrier, len(partners))

    def row_block(base, count):
        return pl.ds(pl.multiple_of(base, 16), count)

    def token_out(j):
        to = plane(ORDER[j])
        src = tokens_hbm.at[row_block(y * quarter, quarter), pl.ds(pl.multiple_of(to * depth, 128), depth)]
        return remote(src, tok.at[z, row_block(y * quarter, quarter), :], tz_s.at[j], tz_r.at[j], at_z(to))

    def token_in(j):
        block = tok.at[plane(-ORDER[j]), row_block(y * quarter, quarter), :]
        return remote(block, block, tz_s.at[j], tz_r.at[j], z_up)

    def token_y(j, kind, incoming):
        s = plane(-ORDER[j])
        me = (yp if kind in (1, 3) else ym) if incoming else y
        base, count = me * quarter, quarter
        if kind >= 2:
            origin = y2 if incoming else (ym if kind == 2 else yp)
            base, count = origin * quarter + (0 if kind == 2 else half_rows), half_rows
        block = tok.at[s, row_block(base, count), :]
        return remote(block, block, ty_s.at[kind], ty_r.at[kind, j], y_up if kind in (0, 2) else y_dn)

    token_out(0).start()
    token_out(2).start()

    def token_next(last, j):
        token_out(last).wait_send()
        token_out(j).start()

    def w_block(k, which):
        return wg.at[k, pl.ds(pl.multiple_of(which * rows, 64), rows), :]

    def w_copy(kind, k, incoming):
        sent = (r, r, r ^ 2)[kind]
        came = (r ^ 1, r ^ 2, r ^ 3)[kind]
        block = w_block(k, came if incoming else sent)
        return remote(block, block, w_s.at[kind], w_r.at[kind, k], other_xl if kind == 1 else other_core)

    for k in range(pairs):
        w_copy(1, k, False).start()
        w_copy(0, k, False).start()

    def take_in(j):
        token_in(j).wait_recv()
        token_y(j, 0, False).start()
        token_y(j, 1, False).start()

    def hand_on(j):
        token_y(j, 0, True).wait_recv()
        token_y(j, 2, False).start()
        token_y(j, 1, True).wait_recv()
        token_y(j, 3, False).start()

    def token_ready(j):
        token_y(j, 2, True).wait_recv()
        token_y(j, 3, True).wait_recv()

    def rs_copy(way, d, k):
        sign = 1 if way == 0 else -1
        src = part.at[k, plane(sign * d)]
        dst = ring.at[way, d - 1, k]
        if d == 4:
            src, dst = src.at[way], dst.at[way]
        return remote(src, dst, rs_s.at[way, d - 1], rs_r.at[way, d - 1, k], z_up if way == 0 else z_dn)

    def products(k, first, second):
        lhs = jnp.concatenate([tok[plane(first)], tok[plane(second)]], axis=0)
        out = dot(lhs, wg[k])
        return [[out[i * length : (i + 1) * length, a * HS : (a + 1) * HS] for a in range(2)] for i in range(2)]

    def weight_on(k):
        w_copy(1, k, True).wait_recv()
        w_copy(2, k, False).start()

    def far_step(k):
        w_copy(0, k, True).wait_recv()
        w_copy(2, k, True).wait_recv()
        far, own = products(k, 4, 0)
        for a in range(2):
            part[k, plane(4), a] = far[a]
            part[k, z, a] = own[a]
        for way in range(2):
            rs_copy(way, 4, k).start()

    token_next(2, 4)
    take_in(2)
    token_next(0, 1)
    take_in(0)
    hand_on(2)
    token_next(4, 6)
    weight_on(0)
    weight_on(1)
    own_tokens.wait()
    hand_on(0)
    token_next(1, 3)
    token_out(5).start()
    take_in(1)
    weight_on(2)
    token_ready(0)
    far_step(0)
    weight_on(3)
    far_step(1)
    hand_on(1)
    far_step(2)
    weight_on(4)
    far_step(3)
    token_ready(2)
    far_step(4)
    for load in loads[1:]:
        load.wait()

    def transpose_tokens(s):
        tok_t[:, pl.ds(pl.multiple_of(s * length, 128), length)] = tok[s].T

    def ring_step(d, k):
        both = products(k, d, -d)
        for way in range(2):
            t = plane(d if way == 0 else -d)
            rs_copy(way, d + 1, k).wait_recv()
            for a in range(2):
                if d == 3 and a != way:
                    part[k, t, a] = both[way][a]
                else:
                    part[k, t, a] = both[way][a] + ring[way, d, k, a]
            rs_copy(way, d, k).start()

    def pair_lanes(k):
        return pl.ds(pl.multiple_of(k * PW, 128), PW)

    def stacked_grads(k):
        grads = dctx_ref[:, pair_lanes(k)]
        return jnp.concatenate([grads[:, :HS], grads[:, HS:]], axis=0)

    token_ready(1)
    for k in range(pairs):
        ring_step(3, k)
        if k == 0:
            take_in(4)
        elif k == 1:
            take_in(6)
            hand_on(4)
        elif k == 2:
            hand_on(6)
            take_in(3)
        elif k == 3:
            take_in(5)
            hand_on(3)
        else:
            hand_on(5)
        wg_t[k * PW : (k + 1) * PW, :] = wg[k].T
    token_ready(3)
    token_ready(4)

    def second_step(k, carry):
        ring_step(2, k)
        transpose_tokens(plane(k + 2))
        return carry

    lax.fori_loop(0, pairs, second_step, 0)
    token_ready(5)
    token_ready(6)

    def third_step(k, carry):
        ring_step(1, k)
        d_probs_ref[k] = dot(stacked_grads(k), values_ref[...], ((1,), (1,)))

        @pl.when(k < 3)
        def _():
            transpose_tokens(plane(k - 1))

        return carry

    lax.fori_loop(0, pairs, third_step, 0)

    scale = 1.0 / HS**0.5
    row_id = lax.broadcasted_iota(jnp.int32, (2, length, length), 1)
    col_id = lax.broadcasted_iota(jnp.int32, (2, length, length), 2)
    causal = (col_id <= row_id).reshape(2 * length, length)
    dk_acc[...] = jnp.zeros_like(dk_acc)
    dv_acc[...] = jnp.zeros_like(dv_acc)

    def ag_copy(way, d, k, incoming):
        sign = -1 if way == 0 else 1
        block = dqall.at[k, plane(sign * (d if incoming else d - 1))]
        if d == 4:
            block = block.at[:, pl.ds(way * HS, HS)]
        return remote(block, block, ag_s.at[way, d - 1], ag_r.at[way, d - 1, k], z_up if way == 0 else z_dn)

    def attention_step(k, carry):
        for way in range(2):
            rs_copy(way, 1, k).wait_recv()
        keys = keys_ref[...]
        q = (part[k, z] + ring[0, 0, k] + ring[1, 0, k]).astype(BF16).reshape(2 * length, HS)
        d_probs = d_probs_ref[k]
        scores = jnp.where(causal, dot(q, keys, ((1,), (1,))) * scale, -1e30)
        e = jnp.exp(scores - jnp.max(scores, axis=-1, keepdims=True))
        probs = e * (1.0 / jnp.sum(e, axis=-1, keepdims=True))
        inner = jnp.sum(d_probs * probs, axis=-1, keepdims=True)
        ds = (probs * (d_probs - inner) * scale).astype(BF16)
        dq = dot(ds, keys).astype(BF16)
        dqall[k, z] = jnp.concatenate([dq[:length], dq[length:]], axis=1)
        for way in range(2):
            ag_copy(way, 1, k, False).start()
        low_ref[k], ds_ref[k], q_ref[k] = probs.astype(BF16), ds, q
        return carry

    lax.fori_loop(0, pairs, attention_step, 0)

    def attention_rest(k):
        low, ds, q = low_ref[k], ds_ref[k], q_ref[k]
        ctx = dot(low, values_ref[...]).astype(BF16)
        ctx_ref[:, pair_lanes(k)] = jnp.concatenate([ctx[:length], ctx[length:]], axis=1)
        dv_acc[...] += dot(low, stacked_grads(k), ((0,), (0,)))
        dk_acc[...] += dot(ds, q, ((0,), (0,)))

    groups = [(0, 1), (1, 2), (3, 2), (5, 2), (7, 1)]
    offsets = (0, -1, 1, -2, 2, -3, 3, 4)
    mid = cols // 2

    def y_copy(g, way, d):
        first, count = groups[g]
        slots = pl.ds(first, count)
        if d == 2:
            src = dts.at[slots, y2, :, pl.ds(way * mid, mid)]
            dst = yr2.at[way, slots]
        else:
            src = dts.at[slots, yp if way == 0 else ym]
            dst = yr1.at[way, slots]
        return remote(src, dst, y_s.at[way, d - 1], y_r.at[way, d - 1, g], y_up if way == 0 else y_dn)

    def d_token_block(g, n):
        first, count = groups[g]
        lhs = jnp.concatenate(
            [
                jnp.concatenate([dqall[k, plane(offsets[first + i])] for k in range(pairs)], axis=1)
                for i in range(count)
            ],
            axis=0,
        )
        lanes = pl.ds(pl.multiple_of(n * PW, 128), PW)
        out = dot(lhs, wg_t[:, lanes]).astype(BF16)
        for i in range(count):
            for owner in range(2 * NY):
                block = out[i * length + owner * 16 : i * length + (owner + 1) * 16]
                dts[first + i, owner % NY, (owner // NY) * 16 : (owner // NY + 1) * 16, lanes] = block

    def y_begin(g):
        for way in range(2):
            y_copy(g, way, 2).start()

    def y_first(g):
        first, count = groups[g]
        for way in range(2):
            y_copy(g, way, 2).wait_recv()
            to = yp if way == 0 else ym
            for i in range(count):
                own = dts[first + i, to, :, way * mid : (way + 1) * mid].astype(F32)
                came = yr2[way, first + i].astype(F32)
                dts[first + i, to, :, way * mid : (way + 1) * mid] = (own + came).astype(BF16)
            y_copy(g, way, 1).start()

    batches = [(0, 3), (3, 2), (5, 3)]

    def x_copy(b):
        first, count = batches[b]
        slots = pl.ds(first, count)
        return remote(red.at[slots, 1 - xh], xr.at[slots], x_s, x_r.at[b], other_xh)

    def y_second(g):
        first, count = groups[g]
        for way in range(2):
            y_copy(g, way, 1).wait_recv()
        for i in range(count):
            slot = first + i
            total = dts[slot, y].astype(F32) + yr1[0, slot].astype(F32) + yr1[1, slot].astype(F32)
            for side in range(2):
                red[slot, side] = total[side * 16 : (side + 1) * 16].astype(BF16)

    def home_copy(slot):
        block = dtk.at[:, pl.ds(pl.multiple_of(z * depth, 128), depth)]
        return remote(fin.at[slot], block, zd_s, zd_r.at[slot], at_z(plane(offsets[slot])))

    def home_in(slot):
        block = dtk.at[:, pl.ds(pl.multiple_of(plane(-offsets[slot]) * depth, 128), depth)]
        return remote(fin.at[slot], block, zd_s, zd_r.at[slot], z_up)

    def x_done(b):
        first, count = batches[b]
        x_copy(b).wait_recv()
        for i in range(count):
            slot = first + i
            total = (red[slot, xh].astype(F32) + xr[slot].astype(F32)).astype(BF16)
            if slot == 0:
                dtk[:, pl.ds(pl.multiple_of(z * depth, 128), depth)] = total
            else:
                fin[slot] = total
                home_copy(slot).start()

    def gc_copy(k):
        return remote(gs.at[k], gcr.at[k], gc_s, gc_r.at[k], other_core)

    def gx_copy(k):
        return remote(gxs.at[k], gxr.at[k], gx_s, gx_r.at[k], other_xl)

    def own_rows(side, core):
        return pl.ds(pl.multiple_of((side * 2 + core) * rows, 64), rows)

    def core_sum(k):
        gc_copy(k).wait_recv()
        away = 1 - xl
        gxs[k] = (ga[k, own_rows(away, c), :] + gcr[k, away].astype(F32)).astype(BF16)
        gx_copy(k).start()

    def grad_block(k):
        ga[k] = dot(tok_t[...], dqall[k].reshape(NZ * length, PW))
        for side in range(2):
            gs[k, side] = ga[k, own_rows(side, 1 - c), :].astype(BF16)
        gc_copy(k).start()

    def gather_step(d, k):
        for way in range(2):
            ag_copy(way, d, k, True).wait_recv()
            if d < 4:
                ag_copy(way, d + 1, k, False).start()

    def d_token_blocks(g, low, high):
        def step(n, carry):
            d_token_block(g, n)
            return carry

        lax.fori_loop(low, high, step, 0)

    def grad_done(k):
        gx_copy(k).wait_recv()
        mine = ga[k, own_rows(xl, c), :] + gcr[k, xl].astype(F32) + gxr[k].astype(F32)
        grad_ref[:, k * PW : (k + 1) * PW] = mine

    early = 2
    for step in range(4 * early):
        d, k = step // early + 1, step % early
        gather_step(d, k)
        if step < pairs:
            attention_rest(step)
            d_token_block(0, step)
        if step == pairs - 1:
            y_begin(0)
        if d == 4:
            grad_block(k)
    dk_ref[...] = dk_acc[...].astype(BF16)
    dv_ref[...] = dv_acc[...].astype(BF16)
    kept = ((ctx_ref, ctx_hbm), (dk_ref, dk_hbm), (dv_ref, dv_hbm))
    stores = [pltpu.make_async_copy(src, dst, out_sem.at[i]) for i, (src, dst) in enumerate(kept)]
    for store in stores:
        store.start()
    y_first(0)
    core_sum(0)
    gather_step(1, 2)
    core_sum(1)
    gather_step(1, 3)
    gather_step(1, 4)
    d_token_blocks(1, 0, pairs)
    y_begin(1)
    for k in range(early, pairs):
        gather_step(2, k)
    d_token_blocks(2, 0, pairs)
    y_begin(2)
    y_second(0)
    gather_step(3, 2)
    gather_step(3, 3)
    y_first(1)
    gather_step(3, 4)
    d_token_blocks(3, 0, pairs)
    y_begin(3)
    gather_step(4, 2)
    grad_block(2)
    y_first(2)
    gather_step(4, 3)
    grad_block(3)
    core_sum(2)
    gather_step(4, 4)
    d_token_blocks(4, 0, pairs)
    y_begin(4)
    y_second(1)
    x_copy(0).start()
    grad_block(4)
    core_sum(3)
    y_first(3)
    core_sum(4)
    y_first(4)
    y_second(2)
    x_copy(1).start()
    x_done(0)
    grad_done(0)
    grad_done(1)
    y_second(3)
    y_second(4)
    x_copy(2).start()
    grad_done(2)
    x_done(1)
    grad_done(3)
    x_done(2)
    grad_done(4)
    grad_store = pltpu.make_async_copy(grad_ref, grad_hbm, out_sem.at[3])
    grad_store.start()
    for slot in range(1, NZ):
        home_in(slot).wait_recv()
    dtok_store = pltpu.make_async_copy(dtk, dtok_hbm, out_sem.at[4])
    dtok_store.start()

    def sent(src, sem):
        remote(src, src, sem, gc_r.at[0], other_core).wait_send()

    for j in (3, 5, 6):
        token_out(j).wait_send()
    for kind in range(4):
        sent(tok.at[pl.ds(0, NZ - 1), pl.ds(0, half_rows if kind >= 2 else quarter), :], ty_s.at[kind])
    for kind in range(3):
        sent(wg.at[:, pl.ds(0, rows), :], w_s.at[kind])
    for way in range(2):
        for d in (1, 2, 3):
            sent(part.at[:, 0], rs_s.at[way, d - 1])
            sent(dqall.at[:, 0], ag_s.at[way, d - 1])
        sent(part.at[:, 0, 0], rs_s.at[way, 3])
        sent(dqall.at[:, 0, :, pl.ds(0, HS)], ag_s.at[way, 3])
        sent(dts.at[:, 0], y_s.at[way, 0])
        sent(dts.at[:, 0, :, pl.ds(0, mid)], y_s.at[way, 1])
    sent(fin.at[pl.ds(1, NZ - 1)], zd_s)
    sent(xr, x_s)
    sent(gs, gc_s)
    sent(gxs, gx_s)
    for store in stores + [grad_store, dtok_store]:
        store.wait()


def fused(tokens, master, keys, values, d_context):
    length, width = tokens.shape
    rows, cols = master.shape
    depth, pairs, mid, quarter = 4 * rows, cols // PW, cols // 2, length // NY
    vmem, dma = pltpu.VMEM, pltpu.SemaphoreType.DMA
    anywhere = pl.BlockSpec(memory_space=pl.ANY)
    return pl.pallas_call(
        kernel,
        out_shape=(
            jax.ShapeDtypeStruct((length, cols), BF16),
            jax.ShapeDtypeStruct((length, HS), BF16),
            jax.ShapeDtypeStruct((length, HS), BF16),
            jax.ShapeDtypeStruct((length // 8, width), BF16),
            jax.ShapeDtypeStruct((rows, cols), F32),
        ),
        in_specs=[anywhere] * 5,
        out_specs=[anywhere] * 5,
        scratch_shapes=[
            vmem((rows, cols), F32),
            vmem((length, HS), BF16),
            vmem((length, HS), BF16),
            vmem((length, cols), BF16),
            vmem((length, cols), BF16),
            vmem((length, HS), BF16),
            vmem((length, HS), BF16),
            vmem((rows, cols), F32),
            vmem((NZ, length, depth), BF16),
            vmem((depth, NZ * length), BF16),
            vmem((pairs, depth, PW), BF16),
            vmem((cols, depth), BF16),
            vmem((pairs, NZ, 2, length, HS), F32),
            vmem((2, 4, pairs, 2, length, HS), F32),
            vmem((pairs, NZ, length, PW), BF16),
            vmem((length, HS), F32),
            vmem((length, HS), F32),
            vmem((pairs, 2 * length, HS), F32),
            vmem((pairs, 2 * length, HS), BF16),
            vmem((pairs, 2 * length, HS), BF16),
            vmem((pairs, 2 * length, HS), BF16),
            vmem((NZ, NY, quarter, depth), BF16),
            vmem((2, NZ, quarter, mid), BF16),
            vmem((2, NZ, quarter, depth), BF16),
            vmem((NZ, 2, 16, depth), BF16),
            vmem((NZ, 16, depth), BF16),
            vmem((NZ, 16, depth), BF16),
            vmem((length // 8, width), BF16),
            vmem((pairs, depth, PW), F32),
            vmem((pairs, 2, rows, PW), BF16),
            vmem((pairs, 2, rows, PW), BF16),
            vmem((pairs, rows, PW), BF16),
            vmem((pairs, rows, PW), BF16),
            dma((4,)),
            dma((5,)),
            dma,
            dma((3,)), dma((3, pairs)),
            dma((NZ - 1,)), dma((NZ - 1,)),
            dma((4,)), dma((4, NZ - 1)),
            dma((2, 4)), dma((2, 4, pairs)),
            dma((2, 4)), dma((2, 4, pairs)),
            dma((2, 2)), dma((2, 2, 5)),
            dma, dma((3,)),
            dma, dma((NZ,)),
            dma, dma((pairs,)),
            dma, dma((pairs,)),
        ],
        compiler_params=pltpu.CompilerParams(
            collective_id=0, has_side_effects=True, vmem_limit_bytes=54 * 1024 * 1024
        ),
    )(tokens, master, keys, values, d_context)


def finish_kernel(*refs):
    wide, small, outs, tidy = refs[:4], refs[4:8], refs[8:11], refs[11:15]
    old, news, held, wide_in, new_out, small_in, small_out = refs[15], refs[16], refs[17:21], *refs[21:]
    parts, rows = old.shape[1], old.shape[2]
    came = [
        [pltpu.make_async_copy(wide[n].at[pl.ds(i * rows, rows)], old.at[n, i], wide_in.at[n, i]) for n in range(4)]
        for i in range(parts)
    ]
    first = [pltpu.make_async_copy(a, b, small_in.at[i]) for i, (a, b) in enumerate(zip(small, held))]
    second = [pltpu.make_async_copy(a, b, small_out.at[i]) for i, (a, b) in enumerate(zip(held, tidy))]
    for copy in came[0] + first + sum(came[1:], []):
        copy.start()
    writes = []
    for i in range(parts):
        for copy in came[i]:
            copy.wait()
        for n, value in enumerate(adam_piece(old[1, i], old[2, i], old[3, i], old[0, i])):
            news[n, i] = value
            writes.append(pltpu.make_async_copy(news.at[n, i], outs[n].at[pl.ds(i * rows, rows)], new_out.at[n, i]))
            writes[-1].start()
        if i == 0:
            for a, b in zip(first, second):
                a.wait()
                b.start()
    for copy in second + writes:
        copy.wait()


def finish(gradient, master, one, two, small):
    rows, cols = master.shape
    parts = 5
    anywhere = pl.BlockSpec(memory_space=pl.ANY)
    vmem, dma = pltpu.VMEM, pltpu.SemaphoreType.DMA
    like = jax.ShapeDtypeStruct((rows, cols), F32)
    return pl.pallas_call(
        finish_kernel,
        out_shape=[like] * 3 + [jax.ShapeDtypeStruct(a.shape, a.dtype) for a in small],
        in_specs=[anywhere] * 8,
        out_specs=[anywhere] * 7,
        scratch_shapes=[vmem((4, parts, rows // parts, cols), F32), vmem((3, parts, rows // parts, cols), F32)]
        + [vmem(a.shape, a.dtype) for a in small]
        + [dma((4, parts)), dma((3, parts)), dma((4,)), dma((4,))],
        compiler_params=pltpu.CompilerParams(vmem_limit_bytes=60 * 1024 * 1024),
    )(gradient, master, one, two, *small)


def body(tokens, master, moment_one, moment_two, keys, values, d_context):
    *small, gradient = fused(tokens, master, keys, values, d_context)
    new_master, new_one, new_two, *small = finish(gradient, master, moment_one, moment_two, small)
    return (*small, new_master, new_one, new_two)


def solution(mesh):
    both = P("node", "local")
    return jax.shard_map(
        body,
        mesh=mesh,
        in_specs=(P("node", None), both, both, both, both, both, both),
        out_specs=(both, both, both, P(("node", "local"), None), both, both, both),
        check_vma=False,
    )
```

time: 169 us -> 156 us (0.923)
  Pallas kernels: 158 us -> 153 us
  other arithmetic: 4.81 us -> 0 us
  local copies, waits for them, and re-layouts: 2.7 us -> 0 us
    pallas_call x1, Pallas kernels: 158 us -> 147 us  [fused(): pl.pallas_call(kernel, out_shape=(jax.ShapeDtypeStruct((length, cols), BF...]
    pallas_call x0 -> x1, Pallas kernels: none -> 5.87 us  [finish(): pl.pallas_call(finish_kernel, out_shape=[like] * 3 + [jax.ShapeDtypeStruc...]
    sub x1 -> x0, other arithmetic: 4.81 us -> none  [adam_piece(): new_master = master - 0.001 * first_hat / (jnp.sqrt(second_hat) + 1e-08)]
    unnamed x16 -> x0, local copies, waits for them, and re-layouts: 2.7 us -> none
where the time goes in v2:
time: 156 us; the launch traced here: 154 us
  Pallas kernels  153 us (98%)
    pallas_call x1, Pallas kernels, fused(): pl.pallas_call(kernel, out_shape=(jax.ShapeDtypeStruct((length, cols), BF...  147 us
    pallas_call x1, Pallas kernels, finish(): pl.pallas_call(finish_kernel, out_shape=[like] * 3 + [jax.ShapeDtypeStruc...  5.87 us

profile of v2, /device:TPU:32, one launch (start us, length us, event | category | flops | bytes accessed | tf_op | source)
XLA Modules:
  0.0 153.5 jit_solution(16236558371831638753)
XLA Ops:
  0.6 146.9 %shard_map.126 = (bf16[128,1280]{1,0:T(8,128)(2,1)}, bf16[128,128]{1,0:T(8,128)(2,1)}, bf16[128,128]{1,0:T(8,128)(2,1)}, bf16[16,10240]{1,0:T(8,128)(2,1)}, f32[320,1280]{1,0:T(8,128)}) custom-call(bf16[128,10240]{1,0:T(8,128)(2,1)} %tokens_hbm.1, f32[320,1280]{1,0:T(8,128)} %refs_1_.1, bf16[128,128]{1,0:T(8,128)(2,1)} %keys_hbm.1, ...), custom_call_target="tpu_custom_call" | custom-call | tf_op jit(solution)/shard_map/pallas_call | solution.py:531
  147.5 5.9 %shard_map.127 = (f32[320,1280]{1,0:T(8,128)}, f32[320,1280]{1,0:T(8,128)}, f32[320,1280]{1,0:T(8,128)}, bf16[128,1280]{1,0:T(8,128)(2,1)}, bf16[128,128]{1,0:T(...) custom-call(f32[320,1280]{1,0:T(8,128)} %get-tuple-element.19.refs_0_, f32[320,1280]{1,0:T(8,128)} %refs_1_.1, ...), custom_call_target="tpu_custom_call" | custom-call | tf_op jit(solution)/shard_map/pallas_call | solution.py:630

commit v3 on v2

--- a/solution.py
+++ b/solution.py
@@ -172,6 +172,9 @@
         for way in range(2):
             rs_copy(way, 4, k).start()
 
+    def transpose_weight(k):
+        wg_t[pl.ds(pl.multiple_of(k * PW, PW), PW), :] = wg[k].T
+
     token_next(2, 4)
     take_in(2)
     token_next(0, 1)
@@ -191,11 +194,13 @@
     weight_on(3)
     far_step(1)
     hand_on(1)
+    transpose_weight(0)
     far_step(2)
     weight_on(4)
     far_step(3)
     token_ready(2)
     far_step(4)
+    transpose_weight(1)
     for load in loads[1:]:
         load.wait()
 
@@ -237,7 +242,6 @@
             hand_on(3)
         else:
             hand_on(5)
-        wg_t[k * PW : (k + 1) * PW, :] = wg[k].T
     token_ready(3)
     token_ready(4)
 
@@ -256,7 +260,11 @@
 
         @pl.when(k < 3)
         def _():
-            transpose_tokens(plane(k - 1))
+            transpose_weight(k + 2)
+
+        @pl.when(k >= 2)
+        def _():
+            transpose_tokens(plane(k - 3))
 
         return carry
 
@@ -425,17 +433,20 @@
         mine = ga[k, own_rows(xl, c), :] + gcr[k, xl].astype(F32) + gxr[k].astype(F32)
         grad_ref[:, k * PW : (k + 1) * PW] = mine
 
-    early = 2
-    for step in range(4 * early):
-        d, k = step // early + 1, step % early
-        gather_step(d, k)
-        if step < pairs:
-            attention_rest(step)
-            d_token_block(0, step)
-        if step == pairs - 1:
-            y_begin(0)
-        if d == 4:
-            grad_block(k)
+    for k in range(pairs):
+        gather_step(1, k)
+        d_token_block(0, k)
+        if k < 2:
+            attention_rest(k)
+    y_begin(0)
+    d_token_blocks(1, 0, pairs)
+    y_begin(1)
+    gather_step(2, 0)
+    attention_rest(2)
+    gather_step(2, 1)
+    attention_rest(3)
+    gather_step(2, 2)
+    attention_rest(4)
     dk_ref[...] = dk_acc[...].astype(BF16)
     dv_ref[...] = dv_acc[...].astype(BF16)
     kept = ((ctx_ref, ctx_hbm), (dk_ref, dk_hbm), (dv_ref, dv_hbm))
@@ -443,50 +454,51 @@
     for store in stores:
         store.start()
     y_first(0)
-    core_sum(0)
-    gather_step(1, 2)
-    core_sum(1)
-    gather_step(1, 3)
-    gather_step(1, 4)
-    d_token_blocks(1, 0, pairs)
-    y_begin(1)
-    for k in range(early, pairs):
-        gather_step(2, k)
+    gather_step(3, 0)
+    gather_step(2, 3)
+    gather_step(3, 1)
+    gather_step(2, 4)
     d_token_blocks(2, 0, pairs)
     y_begin(2)
+    y_first(1)
+    gather_step(3, 2)
+    gather_step(4, 0)
+    grad_block(0)
     y_second(0)
-    gather_step(3, 2)
     gather_step(3, 3)
-    y_first(1)
+    gather_step(4, 1)
+    grad_block(1)
+    core_sum(0)
     gather_step(3, 4)
     d_token_blocks(3, 0, pairs)
     y_begin(3)
+    y_first(2)
+    y_second(1)
+    x_copy(0).start()
     gather_step(4, 2)
     grad_block(2)
-    y_first(2)
+    core_sum(1)
     gather_step(4, 3)
     grad_block(3)
     core_sum(2)
     gather_step(4, 4)
     d_token_blocks(4, 0, pairs)
     y_begin(4)
-    y_second(1)
-    x_copy(0).start()
+    y_second(2)
+    x_copy(1).start()
     grad_block(4)
     core_sum(3)
     y_first(3)
     core_sum(4)
     y_first(4)
-    y_second(2)
-    x_copy(1).start()
     x_done(0)
     grad_done(0)
+    y_second(3)
     grad_done(1)
-    y_second(3)
     y_second(4)
     x_copy(2).start()
+    x_done(1)
     grad_done(2)
-    x_done(1)
     grad_done(3)
     x_done(2)
     grad_done(4)

time: 156 us -> 149 us (0.955); the launches traced: 154 us -> 149 us
  Pallas kernels: 153 us -> 148 us
    pallas_call x1, Pallas kernels: 147 us -> 142 us  [fused(): pl.pallas_call(kernel, out_shape=(jax.ShapeDtypeStruct((length, cols), BF...]
where the time goes in v3:
time: 149 us
  Pallas kernels  148 us (99%)
    pallas_call x1, Pallas kernels, fused(): pl.pallas_call(kernel, out_shape=(jax.ShapeDtypeStruct((length, cols), BF...  142 us
    pallas_call x1, Pallas kernels, finish(): pl.pallas_call(finish_kernel, out_shape=[like] * 3 + [jax.ShapeDtypeStruc...  5.87 us

profile of v3, /device:TPU:32, one launch (start us, length us, event | category | flops | bytes accessed | tf_op | source)
XLA Modules:
  0.0 148.6 jit_solution(5649016866369720096)
XLA Ops:
  0.6 141.9 %shard_map.126 = (bf16[128,1280]{1,0:T(8,128)(2,1)}, bf16[128,128]{1,0:T(8,128)(2,1)}, bf16[128,128]{1,0:T(8,128)(2,1)}, bf16[16,10240]{1,0:T(8,128)(2,1)}, f32[320,1280]{1,0:T(8,128)}) custom-call(bf16[128,10240]{1,0:T(8,128)(2,1)} %tokens_hbm.1, f32[320,1280]{1,0:T(8,128)} %refs_1_.1, bf16[128,128]{1,0:T(8,128)(2,1)} %keys_hbm.1, ...), custom_call_target="tpu_custom_call" | custom-call | tf_op jit(solution)/shard_map/pallas_call | solution.py:543
  142.6 5.9 %shard_map.127 = (f32[320,1280]{1,0:T(8,128)}, f32[320,1280]{1,0:T(8,128)}, f32[320,1280]{1,0:T(8,128)}, bf16[128,1280]{1,0:T(8,128)(2,1)}, bf16[128,128]{1,0:T(...) custom-call(f32[320,1280]{1,0:T(8,128)} %get-tuple-element.19.refs_0_, f32[320,1280]{1,0:T(8,128)} %refs_1_.1, ...), custom_call_target="tpu_custom_call" | custom-call | tf_op jit(solution)/shard_map/pallas_call | solution.py:642

commit v4 on v3

--- a/solution.py
+++ b/solution.py
@@ -476,33 +476,36 @@
     y_second(1)
     x_copy(0).start()
     gather_step(4, 2)
-    grad_block(2)
-    core_sum(1)
     gather_step(4, 3)
-    grad_block(3)
-    core_sum(2)
     gather_step(4, 4)
     d_token_blocks(4, 0, pairs)
     y_begin(4)
+    core_sum(1)
+    grad_block(2)
+    grad_block(3)
+    core_sum(2)
     y_second(2)
     x_copy(1).start()
+    y_first(3)
+    core_sum(3)
     grad_block(4)
-    core_sum(3)
-    y_first(3)
+    y_first(4)
     core_sum(4)
-    y_first(4)
-    x_done(0)
-    grad_done(0)
     y_second(3)
-    grad_done(1)
     y_second(4)
     x_copy(2).start()
+    x_done(0)
     x_done(1)
+    grad_done(0)
+    grad_done(1)
     grad_done(2)
     grad_done(3)
+    ahead, last = pl.ds(0, cols - PW), pl.ds(cols - PW, PW)
+    most_store = pltpu.make_async_copy(grad_ref.at[:, ahead], grad_hbm.at[:, ahead], out_sem.at[3])
+    most_store.start()
     x_done(2)
     grad_done(4)
-    grad_store = pltpu.make_async_copy(grad_ref, grad_hbm, out_sem.at[3])
+    grad_store = pltpu.make_async_copy(grad_ref.at[:, last], grad_hbm.at[:, last], out_sem.at[5])
     grad_store.start()
     for slot in range(1, NZ):
         home_in(slot).wait_recv()
@@ -530,7 +533,7 @@
     sent(xr, x_s)
     sent(gs, gc_s)
     sent(gxs, gx_s)
-    for store in stores + [grad_store, dtok_store]:
+    for store in stores + [most_store, grad_store, dtok_store]:
         store.wait()
 
 
@@ -586,7 +589,7 @@
             vmem((pairs, rows, PW), BF16),
             vmem((pairs, rows, PW), BF16),
             dma((4,)),
-            dma((5,)),
+            dma((6,)),
             dma,
             dma((3,)), dma((3, pairs)),
             dma((NZ - 1,)), dma((NZ - 1,)),

time: 149 us -> 148 us (level)
  no operation moved by 1% of the time
where the time goes in v4:
time: 148 us
  Pallas kernels  147 us (99%)
    pallas_call x1, Pallas kernels, fused(): pl.pallas_call(kernel, out_shape=(jax.ShapeDtypeStruct((length, cols), BF...  141 us
    pallas_call x1, Pallas kernels, finish(): pl.pallas_call(finish_kernel, out_shape=[like] * 3 + [jax.ShapeDtypeStruc...  5.87 us

profile of v4, /device:TPU:32, one launch (start us, length us, event | category | flops | bytes accessed | tf_op | source)
XLA Modules:
  0.0 147.8 jit_solution(7864416806799476354)
XLA Ops:
  0.6 141.1 %shard_map.126 = (bf16[128,1280]{1,0:T(8,128)(2,1)}, bf16[128,128]{1,0:T(8,128)(2,1)}, bf16[128,128]{1,0:T(8,128)(2,1)}, bf16[16,10240]{1,0:T(8,128)(2,1)}, f32[320,1280]{1,0:T(8,128)}) custom-call(bf16[128,10240]{1,0:T(8,128)(2,1)} %tokens_hbm.1, f32[320,1280]{1,0:T(8,128)} %refs_1_.1, bf16[128,128]{1,0:T(8,128)(2,1)} %keys_hbm.1, ...), custom_call_target="tpu_custom_call" | custom-call | tf_op jit(solution)/shard_map/pallas_call | solution.py:546
  141.8 5.9 %shard_map.127 = (f32[320,1280]{1,0:T(8,128)}, f32[320,1280]{1,0:T(8,128)}, f32[320,1280]{1,0:T(8,128)}, bf16[128,1280]{1,0:T(8,128)(2,1)}, bf16[128,128]{1,0:T(...) custom-call(f32[320,1280]{1,0:T(8,128)} %get-tuple-element.19.refs_0_, f32[320,1280]{1,0:T(8,128)} %refs_1_.1, ...), custom_call_target="tpu_custom_call" | custom-call | tf_op jit(solution)/shard_map/pallas_call | solution.py:645
